TPU v7x, 1024 devices: a whole 4x8x16 slice. The times are simulated.
1024 devices in a mesh: dp: 4 (over z_hi), expert: 32 (over x, y), tensor: 8 (over z_lo, core).
Axes of the slice: x: 4, y: 8, z: 16 (z_hi: 4, z_lo: 4; z = z_hi * 4 + z_lo), core: 2. Of those that a mesh axis runs over, the one named last changes fastest.
Arguments:
- context: bfloat16 [32768, 4096], P(('dp', 'expert'), 'tensor'), parts along dimension 0, may hold values from -6 to 6
- out_weight: bfloat16 [4096, 7168], P('tensor'), may hold values from -0.09375 to 0.09375
- attn_bias: bfloat16 [7168], replicated, may hold values from -3 to 3
- residual: bfloat16 [32768, 7168], P(('dp', 'expert', 'tensor')), parts along dimension 0, may hold values from -6 to 6
- dropout_bits: int32 [32768, 448], P(('dp', 'expert', 'tensor')), parts along dimension 0, may hold values from 0 to 65535, as said below
- norm_gain: bfloat16 [7168], replicated, may hold values from 0.5 to 1.5
- routes: int32 [32768, 2], P(('dp', 'expert', 'tensor')), parts along dimension 0, may hold values from 0 to 63, all different within a row; in each aligned block of 32 rows (0 to 31, 32 to 63, ...) at most 2 rows name the same one
Outputs:
- hidden_state: bfloat16 [32768, 7168], P(('dp', 'expert', 'tensor')), parts along dimension 0
- dispatched: bfloat16 [128, 8, 64, 2, 7168], P('dp', 'tensor', 'expert'), parts along dimension 0
There are 4 independent parts, one for each index of `dp`. A program takes and returns all parts, laid end to end along the dimension named above; an argument that names none is the same for every part. Nothing has to cross between parts.
Inputs may be any that keep to these rules, and one draw needn't show every extreme that they name: `routes`: each row names two different experts; within the 32 rows of one device no expert is named more than 2 times. `dropout_bits`: bit b of word w of a row is 1 where feature 16 w + b is kept; each word uses its 16 lowest bits.
All inputs are finite; a program needn't handle non-finite values.
Results may differ from a plain program's by a relative error of at most 0.015.
Values may be sent and summed in bfloat16 or wider, within the bound.
A program may use at most 64 MiB of HBM per device.

v0:
```python
import jax
import jax.numpy as jnp
from jax import lax
from jax.sharding import PartitionSpec as P

E_DEV = 2


keep_scale = 1.0 / 0.9
eps_norm = 1e-05


def local(context, out_weight, attn_bias, residual, dropout_bits, norm_gain, routes):
    token_rows = residual.shape[0]
    feature_count = residual.shape[1]
    partial_value = jnp.dot(context, out_weight, preferred_element_type=jnp.float32)
    attention = lax.psum_scatter(
        partial_value.astype(jnp.bfloat16), "tensor", scatter_dimension=0, tiled=True
    )
    word_rows = jnp.repeat(dropout_bits, 16, axis=1)
    offsets = lax.broadcasted_iota(jnp.int32, word_rows.shape, 1) % 16
    keep_mask = jnp.bitwise_and(jnp.right_shift(word_rows, offsets), 1).astype(jnp.float32)
    hidden_state = (
        residual.astype(jnp.float32)
        + keep_mask * (attention.astype(jnp.float32) + attn_bias.astype(jnp.float32)) * keep_scale
    ).astype(jnp.bfloat16)
    hidden_float = hidden_state.astype(jnp.float32)
    mean_square = jnp.mean(hidden_float * hidden_float, axis=-1, keepdims=True)
    normed = (
        hidden_float * lax.rsqrt(mean_square + eps_norm) * norm_gain.astype(jnp.float32)
    ).astype(jnp.bfloat16)
    owners = lax.axis_size("expert")
    experts_all = E_DEV * owners
    capacity = 4 * token_rows // experts_all
    flat_routes = routes.reshape(-1)
    onehot = (flat_routes[:, None] == jnp.arange(experts_all, dtype=jnp.int32)[None, :]).astype(
        jnp.int32
    )
    earlier = jnp.cumsum(onehot, axis=0) - onehot
    slot_index = jnp.sum(earlier * onehot, axis=1)
    positions = (flat_routes * capacity + slot_index).reshape(token_rows, 2)
    targets = jnp.arange(experts_all * capacity, dtype=jnp.int32)
    select = jnp.sum(
        (positions[None, :, :] == targets[:, None, None]).astype(jnp.int32), axis=2
    ).astype(jnp.bfloat16)
    buffer = jnp.dot(select, normed, preferred_element_type=jnp.float32).astype(jnp.bfloat16)
    buffer = buffer.reshape(owners, E_DEV, capacity, feature_count)
    received = lax.all_to_all(buffer, "expert", split_axis=0, concat_axis=0, tiled=True)
    dispatched = received[:, None]
    return (hidden_state, dispatched)


def solution(mesh):
    placed = (
        P(("dp", "expert"), "tensor"),
        P("tensor", None),
        P(),
        P(("dp", "expert", "tensor"), None),
        P(("dp", "expert", "tensor"), None),
        P(),
        P(("dp", "expert", "tensor"), None),
    )
    return jax.shard_map(
        local,
        mesh=mesh,
        in_specs=placed,
        out_specs=(P(("dp", "expert", "tensor"), None), P("dp", "tensor", "expert", None, None)),
        check_vma=False,
    )
```

profile of v0, /device:TPU:8, one launch (start us, length us, event | category | flops | bytes accessed | tf_op | source)
XLA Modules:
  0.0 146.4 jit_solution(10779007765563802874)
XLA Ops:
  7.2 0.0 copy-start
  7.2 0.0 reduce-scatter.2.cloned.1.call-start
  7.2 0.9 copy-done
  8.1 7.0 %convolution_convert_fusion = bf16[256,7168]{1,0:T(8,128)(2,1)} fusion(bf16[256,512]{1,0:T(8,128)(2,1)S(1)} %copy-done, bf16[512,7168]{1,0:T(8,128)(2,1)} %param.8), kind=kOutput, calls=%fused_computation | convolution fusion | flops 1880883200 | bytes 11272192 | tf_op jit(solution)/shard_map/dot_general | solution.py:16
  15.1 0.0 reduce-scatter.2.cloned.1.call-update
  15.1 0.7 copy-done.4
  15.8 0.1 copy-done.3
  16.0 0.1 copy.23
  16.1 2.1 %broadcast_in_dim.4 = s32[32,448,16]{0,2,1:T(8,128)} broadcast(s32[32,448]{0,1:T(8,128)S(1)} %copy.23), dimensions={0,1} | broadcast | bytes 974848 | tf_op jit(solution)/shard_map/broadcast_in_dim | solution.py:20
  18.2 2.6 %copy.24 = s32[32,7168]{1,0:T(8,128)S(1)} copy(s32[32,7168]{0,1:T(8,128)} %bitcast.4) | data formatting | bytes 1835008 | tf_op jit(solution)/shard_map/reshape | solution.py:20
  20.8 0.1 copy.25
  20.9 0.1 eq.30
  21.0 0.1 fusion.6
  21.1 0.1 reduce_window_sum.11
  21.2 0.2 select_reduce_fusion
  21.3 0.1 reduce_sum.30
  21.5 0.1 copy.26
  21.6 0.1 convert_reduce_fusion
  21.6 60.1 %reduce-scatter.2.cloned.1.call-done = bf16[32,7168]{1,0:T(8,128)(2,1)} async-done(((bf16[256,7168]{1,0:T(8,128)(2,1)}), bf16[32,7168]{1,0:T(8,128)(2,1)}) %reduce-scatter.2.cloned.1.call-update) | async-done | bytes 458768 | tf_op jit(solution)/shard_map/reduce_scatter | solution.py:17
  81.7 1.5 %fusion = (f32[32]{0:T(128)S(1)}, bf16[32,7168]{1,0:T(8,128)(2,1)S(1)}) fusion(f32[7168]{0:T(1024)S(1)} %convert_element_type.43, bf16[32,7168]{1,0:T(8,128)(2,1)} %reduce-scatter.2.cloned.1.call-done, s32[32,7168]{1,0:T(8,128)S(1)} %copy.24, s32[7168]{0:T(1024)S(1)} %get-tuple-element.4, s32[7168]{0:T(1024)S(1)} %get-tuple-element.5, ...), kind=kLoop, calls=%fused_computation.4 | loop fusion | flops 3211232 | bytes 2387072 | tf_op jit(solution)/shard_map/reduce_sum | solution.py:28
  83.2 0.7 convolution_convert_fusion.1
  83.9 1.6 %reshape.29 = bf16[32,2,2,7168]{3,2,1,0:T(2,128)(2,1)} reshape(bf16[128,7168]{1,0:T(8,128)(2,1)S(1)} %convolution_convert_fusion.1) | data formatting | bytes 3670016 | tf_op jit(solution)/shard_map/reshape | solution.py:47
  85.6 52.7 %all_to_all.5 = bf16[32,2,2,7168]{3,2,1,0:T(2,128)(2,1)S(1)} all-to-all(bf16[32,2,2,7168]{3,2,1,0:T(2,128)(2,1)} %reshape.29), channel_id=1, replica_groups=mesh['dp'=4,'expert'=32,'tensor'=8] {'expert'}, dimensions={0} | all-to-all | bytes 3670016 | tf_op jit(solution)/shard_map/all_to_all | solution.py:48
  138.3 1.2 copy.28
  (16 shorter events, 0.1 us)
Async XLA Ops:
  7.2 1.0 copy-start
  7.2 74.5 %reduce-scatter.2.cloned.1.call-start = ((), (), s32[]{:S(2)}) async-start(), calls=%async_computation.2 | async-start | bytes 4128768 | tf_op jit(solution)/shard_map/reduce_scatter | solution.py:17
  15.1 0.7 copy-start.4
  15.1 0.9 copy-start.3
  16.1 4.7 %copy-start.5 = (bf16[7168]{0:T(1024)(128)(2,1)S(1)}, bf16[7168]{0:T(1024)(128)(2,1)}, u32[]{:S(2)}) copy-start(bf16[7168]{0:T(1024)(128)(2,1)} %param.12) | copy-start | bytes 43012
  16.1 4.7 %copy-start.6 = (s32[32,2]{0,1:T(2,128)S(1)}, s32[32,2]{0,1:T(2,128)}, u32[]{:S(2)}) copy-start(s32[32,2]{0,1:T(2,128)} %param.13) | copy-start | bytes 772
  16.1 65.6 %copy-start.2 = (bf16[32,7168]{1,0:T(8,128)(2,1)S(1)}, bf16[32,7168]{1,0:T(8,128)(2,1)}, u32[]{:S(2)}) copy-start(bf16[32,7168]{1,0:T(8,128)(2,1)} %param.10) | copy-start | bytes 1376260
  83.2 55.1 %copy-start.1 = (bf16[32,7168]{1,0:T(8,128)(2,1)}, bf16[32,7168]{1,0:T(8,128)(2,1)S(1)}, u32[]{:S(2)}) copy-start(bf16[32,7168]{1,0:T(8,128)(2,1)S(1)} %get-tuple-element.8) | copy-start | bytes 1376260
Sparse Core Ops, SparseCore 0:
  15.2 66.4 reduce-scatter.1
where the time goes:
time: 147 us; the launch traced here: 146 us
  waiting for transfers between devices  60.1 us (41%)
  blocking collectives  52.7 us (36%)
  between operations  14.2 us (10%)
  local copies, waits for them, and re-layouts  9.74 us (7%)
  matrix products  7.66 us (5%)
  other arithmetic  1.97 us (1%)
    reduce_scatter x1, waiting for transfers between devices, local(): lax.psum_scatter(partial_value.astype(jnp.bfloat16), 'tensor', scatter_di...  60.1 us
    all_to_all x1, blocking collectives, local(): lax.all_to_all(buffer, 'expert', split_axis=0, concat_axis=0, tiled=True)  52.7 us
    dot_general x1, matrix products, local(): jnp.dot(context, out_weight, preferred_element_type=jnp.float32)  6.98 us
    unnamed x17, local copies, waits for them, and re-layouts  3.19 us
  transfers between devices with their start and end apart: 1, of which 1 were waited for; matrix products, arithmetic and copies ran while one was open for 4% of the time, Pallas kernels for 0%

commit v1 on v0

v1 whole, which is shorter than its diff:
```python
import functools

import jax
import jax.numpy as jnp
from jax import lax
from jax.experimental import pallas as pl
from jax.experimental.pallas import tpu as pltpu
from jax.sharding import PartitionSpec as P

MESH = pl.DeviceIdType.MESH
KEEP_SCALE = 1.0 / 0.9
EPS = 1e-05
BF16 = jnp.bfloat16
F32 = jnp.float32

STRIP = 256


def iota(shape, dim):
    return lax.broadcasted_iota(jnp.int32, shape, dim)


def kernel(
    owners, groups, features,
    ctx_hbm, w_hbm, bias_ref, res_hbm, bits_hbm, routes_ref,
    hid_hbm, raw_hbm, scl_hbm,
    ctx_s, w_s, a_send, a_own, a_recv, b_send, b_recv, b_keep, c_send, c_recv, c_keep,
    res_s, bits_s, mask_s, hid_s, select_s, slots_s, squares_s, x_send, scl_s,
    ctx_sem, w_sem, res_sem, bits_sem, hid_sem, own_sem, own_scl_sem,
    a_ssem, a_rsem, b_ssem, b_rsem, c_ssem, c_rsem, x_ssem, x_rsem, s_ssem, s_rsem,
):
    quarter = features // 4
    chunks = quarter // STRIP
    expert = lax.axis_index("expert")
    tensor = lax.axis_index("tensor")
    chip = tensor // 2
    core = tensor % 2
    sibling = chip * 2 + (1 - core)
    chip1 = chip + 1 - 2 * (chip % 2)
    chip2 = (chip + 2) % 4
    chip3 = 3 - chip
    partner1 = chip1 * 2 + core
    partner2 = chip2 * 2 + core

    barrier = pltpu.get_barrier_semaphore()
    for peer in (sibling, partner1, partner2):
        pl.semaphore_signal(barrier, inc=1, device_id={"tensor": peer}, device_id_type=MESH)

    @pl.loop(1, owners)
    def _(i):
        peer = (expert + i) % owners
        pl.semaphore_signal(barrier, inc=1, device_id={"expert": peer}, device_id_type=MESH)

    ctx_copies = []
    for half, c_own in ((0, 1 - core), (1, core)):
        for place, dest in enumerate((chip3, chip1, chip2, chip)):
            rows = pl.ds(pl.multiple_of((dest * 2 + c_own) * 32, 32), 32)
            ctx_copies.append(
                pltpu.make_async_copy(
                    ctx_hbm.at[rows, :],
                    ctx_s.at[pl.ds(half * 128 + place * 32, 32), :],
                    ctx_sem.at[half * 4 + place],
                )
            )
    for copy in ctx_copies:
        copy.start()

    def w_copy(k, q):
        cols = pl.ds(pl.multiple_of(q * quarter + k * STRIP, 128), STRIP)
        return pltpu.make_async_copy(
            w_hbm.at[:, cols], w_s.at[k, :, pl.ds(q * STRIP, STRIP)], w_sem.at[k, q]
        )

    @pl.loop(0, chunks)
    def _(k):
        for q in range(4):
            w_copy(k, q).start()

    res_copy = pltpu.make_async_copy(res_hbm, res_s, res_sem)
    res_copy.start()
    bits_copy = pltpu.make_async_copy(bits_hbm, bits_s, bits_sem)
    bits_copy.start()

    def matmul(k):
        for q in range(4):
            w_copy(k, q).wait()
        part = jnp.dot(ctx_s[...], w_s[k], preferred_element_type=F32).astype(BF16)
        a_send[k] = part[:128]
        a_own[k] = part[128:]

    def remote(src, dst, ssem, rsem, peer):
        return pltpu.make_async_remote_copy(
            src_ref=src, dst_ref=dst, send_sem=ssem, recv_sem=rsem,
            device_id={"tensor": peer}, device_id_type=MESH,
        )

    def a_copy(k):
        return remote(a_send.at[k], a_recv.at[k], a_ssem.at[k], a_rsem.at[k], sibling)

    def b_copy(k):
        return remote(b_send.at[k], b_recv.at[k], b_ssem.at[k], b_rsem.at[k], partner1)

    def c_copy(k):
        return remote(c_send.at[k], c_recv.at[k], c_ssem.at[k], c_rsem.at[k], partner2)

    def stage_b(k):
        a_copy(k).wait_recv()
        b_send[k] = (a_own[k, :64].astype(F32) + a_recv[k, :64].astype(F32)).astype(BF16)
        b_copy(k).start()
        b_keep[k] = a_own[k, 64:].astype(F32) + a_recv[k, 64:].astype(F32)

    def stage_c(k):
        b_copy(k).wait_recv()
        c_send[k] = (b_keep[k, :32] + b_recv[k, :32].astype(F32)).astype(BF16)
        c_copy(k).start()
        c_keep[k] = b_keep[k, 32:] + b_recv[k, 32:].astype(F32)

    def stage_x(k):
        c_copy(k).wait_recv()
        pieces = []
        for q in range(4):
            cols = pl.ds(pl.multiple_of(q * quarter + k * STRIP, 128), STRIP)
            lanes = pl.ds(q * STRIP, STRIP)
            total = c_keep[k, :, lanes] + c_recv[k, :, lanes].astype(F32)
            attention = total.astype(BF16).astype(F32)
            hidden = (
                res_s[:, cols].astype(F32)
                + (attention + bias_ref[:, cols].astype(F32)) * mask_s[:, cols]
            ).astype(BF16)
            hid_s[:, cols] = hidden
            value = hidden.astype(F32)
            square = value * value
            folded = square[:, :128]
            for i in range(1, STRIP // 128):
                folded = folded + square[:, i * 128:(i + 1) * 128]
            squares_s[...] += folded
            pieces.append(hidden)
        stacked = jnp.concatenate(pieces, axis=0)
        picked = jnp.dot(select_s[...], stacked, preferred_element_type=F32).astype(BF16)
        cols = pl.ds(pl.multiple_of(k * STRIP, 128), STRIP)
        x_send[:, :, cols] = picked.reshape(owners, 16, STRIP)

        @pl.loop(1, owners)
        def _(i):
            peer = (expert + i) % owners
            pltpu.make_async_remote_copy(
                src_ref=x_send.at[peer, :, cols], dst_ref=raw_hbm.at[expert, :, cols],
                send_sem=x_ssem, recv_sem=x_rsem,
                device_id={"expert": peer}, device_id_type=MESH,
            ).start()

    for copy in ctx_copies:
        copy.wait()
    matmul(0)
    pl.semaphore_wait(barrier, owners + 2)
    a_copy(0).start()
    matmul(1)
    a_copy(1).start()
    stage_b(0)

    same_token = iota((32, 128), 1) % 32 == iota((32, 128), 0)
    first = jnp.sum(jnp.where(same_token, routes_ref[:, 0:1], 0), axis=0, keepdims=True)
    second = jnp.sum(jnp.where(same_token, routes_ref[:, 1:2], 0), axis=0, keepdims=True)
    j0, j1 = iota((128, 128), 0), iota((128, 128), 1)
    before = jnp.where((j0 // 32 == j1 // 32) & (j0 % 32 < j1 % 32), 1.0, 0.0).astype(BF16)

    def chosen(named, slot):
        hits = jnp.where((first == named) | (second == named), 1.0, 0.0)
        earlier = jnp.dot(hits.astype(BF16), before, preferred_element_type=F32)
        return jnp.where(earlier == slot.astype(F32), hits, 0.0)

    row, lane = iota((owners * 16, 128), 0), iota((owners * 16, 128), 1)
    picks = chosen(2 * (row // 16) + (row % 4) // 2, row % 2)
    select_s[...] = jnp.where((row // 4) % 4 == lane // 32, picks, 0.0).astype(BF16)
    row, lane = iota((owners, 128), 0), iota((owners, 128), 1)
    for slot in range(4):
        picks = chosen(2 * row + slot // 2, jnp.full((owners, 128), slot % 2, jnp.int32))
        slots_s[slot] = jnp.where(lane < 32, picks, 0.0)

    bits_copy.wait()
    squares_s[...] = jnp.zeros_like(squares_s)
    words = features // 16
    for start in range(0, words, 128):
        count = min(128, words - start)
        block = bits_s[:, start:start + count]
        low = (block % 256).astype(F32).astype(BF16)
        high = (block // 256).astype(F32).astype(BF16)
        spread_row, spread_col = iota((count, count * 16), 0), iota((count, count * 16), 1)
        here = spread_col // 16 == spread_row
        is_low = spread_col % 16 < 8
        spread_low = jnp.where(here & is_low, 1.0, 0.0).astype(BF16)
        spread_high = jnp.where(here & jnp.logical_not(is_low), 1.0, 0.0).astype(BF16)
        byte = jnp.dot(low, spread_low, preferred_element_type=F32) + jnp.dot(
            high, spread_high, preferred_element_type=F32
        )
        shift = iota(byte.shape, 1) % 8
        bit = jnp.bitwise_and(jnp.right_shift(byte.astype(jnp.int32), shift), 1)
        mask_s[:, start * 16:(start + count) * 16] = bit.astype(F32) * KEEP_SCALE
    res_copy.wait()

    @pl.loop(0, chunks + 1)
    def _(t):
        @pl.when(t >= 1)
        def _():
            stage_x(t - 1)

        @pl.when(t < chunks)
        def _():
            stage_c(t)

        @pl.when(t + 1 < chunks)
        def _():
            stage_b(t + 1)

        @pl.when(t + 2 < chunks)
        def _():
            matmul(t + 2)
            a_copy(t + 2).start()

    mean = jnp.sum(squares_s[...], axis=1, keepdims=True) / features
    scale = lax.rsqrt(mean + EPS)
    scale_row = jnp.sum(jnp.where(same_token, scale, 0.0), axis=0, keepdims=True)
    packed = jnp.zeros((owners, 128), F32)
    for slot in range(4):
        value = jnp.sum(slots_s[slot] * scale_row, axis=1, keepdims=True)
        packed = packed + jnp.where(lane == slot, value, 0.0)
    scl_s[...] = packed.reshape(owners, 1, 128)

    @pl.loop(1, owners)
    def _(i):
        peer = (expert + i) % owners
        pltpu.make_async_remote_copy(
            src_ref=scl_s.at[peer], dst_ref=scl_hbm.at[expert],
            send_sem=s_ssem, recv_sem=s_rsem,
            device_id={"expert": peer}, device_id_type=MESH,
        ).start()

    hid_copy = pltpu.make_async_copy(hid_s, hid_hbm, hid_sem)
    hid_copy.start()
    own_copy = pltpu.make_async_copy(x_send.at[expert], raw_hbm.at[expert], own_sem)
    own_copy.start()
    own_scl = pltpu.make_async_copy(scl_s.at[expert], scl_hbm.at[expert], own_scl_sem)
    own_scl.start()

    @pl.loop(0, chunks)
    def _(k):
        a_copy(k).wait_send()
        b_copy(k).wait_send()
        c_copy(k).wait_send()

    others = pl.ds(0, owners - 1)
    pltpu.make_async_copy(x_send.at[others], x_send.at[others], x_ssem).wait()
    pltpu.make_async_copy(scl_s.at[others], scl_s.at[others], s_ssem).wait()
    pltpu.make_async_copy(raw_hbm.at[others], raw_hbm.at[others], x_rsem).wait()
    pltpu.make_async_copy(scl_hbm.at[others], scl_hbm.at[others], s_rsem).wait()
    hid_copy.wait()
    own_copy.wait()
    own_scl.wait()


def local(owners, groups, context, out_weight, attn_bias, residual, dropout_bits, norm_gain, routes):
    depth, features = out_weight.shape
    rows = context.shape[0]
    tokens = residual.shape[0]
    quarter = features // 4
    chunks = quarter // STRIP
    wide = 4 * STRIP
    vmem, dma = pltpu.VMEM, pltpu.SemaphoreType.DMA
    hidden, raw, scales = pl.pallas_call(
        functools.partial(kernel, owners, groups, features),
        out_shape=(
            jax.ShapeDtypeStruct((tokens, features), BF16),
            jax.ShapeDtypeStruct((owners, 16, quarter), BF16),
            jax.ShapeDtypeStruct((owners, 1, 128), F32),
        ),
        in_specs=[
            pl.BlockSpec(memory_space=pl.ANY),
            pl.BlockSpec(memory_space=pl.ANY),
            pl.BlockSpec(memory_space=pltpu.VMEM),
            pl.BlockSpec(memory_space=pl.ANY),
            pl.BlockSpec(memory_space=pl.ANY),
            pl.BlockSpec(memory_space=pltpu.VMEM),
        ],
        out_specs=[pl.BlockSpec(memory_space=pl.ANY)] * 3,
        scratch_shapes=[
            vmem((rows, depth), BF16),
            vmem((chunks, depth, wide), BF16),
            vmem((chunks, 128, wide), BF16),
            vmem((chunks, 128, wide), BF16),
            vmem((chunks, 128, wide), BF16),
            vmem((chunks, 64, wide), BF16),
            vmem((chunks, 64, wide), BF16),
            vmem((chunks, 64, wide), F32),
            vmem((chunks, 32, wide), BF16),
            vmem((chunks, 32, wide), BF16),
            vmem((chunks, 32, wide), F32),
            vmem((tokens, features), BF16),
            vmem((tokens, features // 16), jnp.int32),
            vmem((tokens, features), F32),
            vmem((tokens, features), BF16),
            vmem((owners * 16, 128), BF16),
            vmem((4, owners, 128), F32),
            vmem((tokens, 128), F32),
            vmem((owners, 16, quarter), BF16),
            vmem((owners, 1, 128), F32),
            dma((8,)),
            dma((chunks, 4)),
            dma, dma, dma, dma, dma,
            dma((chunks,)), dma((chunks,)),
            dma((chunks,)), dma((chunks,)),
            dma((chunks,)), dma((chunks,)),
            dma, dma, dma, dma,
        ],
        compiler_params=pltpu.CompilerParams(
            collective_id=0, has_side_effects=True, vmem_limit_bytes=48 * 1024 * 1024
        ),
        cost_estimate=pl.CostEstimate(
            flops=2 * rows * depth * features,
            bytes_accessed=2 * depth * features,
            transcendentals=0,
        ),
    )(context, out_weight, attn_bias.reshape(1, -1), residual, dropout_bits, routes)
    placed = raw.reshape(owners, 4, 4, quarter).transpose(0, 2, 1, 3).reshape(owners, 4, features)
    scale = scales[:, 0, :4]
    normed = (
        placed.astype(F32) * scale[:, :, None] * norm_gain.astype(F32)[None, None, :]
    ).astype(BF16)
    return hidden, normed.reshape(owners, 1, 2, 2, features)


def solution(mesh):
    owners, groups = mesh.shape["expert"], mesh.shape["tensor"]
    tokens_split = P(("dp", "expert", "tensor"), None)
    return jax.shard_map(
        functools.partial(local, owners, groups),
        mesh=mesh,
        in_specs=(
            P(("dp", "expert"), "tensor"), P("tensor", None), P(),
            tokens_split, tokens_split, P(), tokens_split,
        ),
        out_specs=(tokens_split, P("dp", "tensor", "expert", None, None)),
        check_vma=False,
    )
```

time: 147 us -> 96.6 us (0.66)
  the two profiles are of different devices: /device:TPU:8 before, /device:TPU:1 now
where the time goes in v1:
time: 96.6 us; the launch traced here: 96 us
  Pallas kernels  71.8 us (74%)
  local copies, waits for them, and re-layouts  18.4 us (19%)
  other arithmetic  5.19 us (5%)
    pallas_call x1, Pallas kernels, local(): pl.pallas_call(functools.partial(kernel, owners, groups, features), out_s...  71.8 us
    convert_element_type x3, local copies, waits for them, and re-layouts, local(): placed.astype(F32) * scale[:, :, None]  13.1 us
    convert_element_type x1, other arithmetic, local(): normed = (placed.astype(F32) * scale[:, :, None] * norm_gain.astype(F32)[...  5.18 us
    unnamed x10, local copies, waits for them, and re-layouts  4.34 us

profile of v1, /device:TPU:1, one launch (start us, length us, event | category | flops | bytes accessed | tf_op | source)
XLA Modules:
  0.0 96.0 jit_solution(13842352404591508999)
XLA Ops:
  0.6 0.7 reshape.37.bias_ref
  1.4 0.8 copy.9.routes_ref
  2.1 0.0 copy-start
  2.1 1.0 %copy-done = bf16[32,7168]{1,0:T(8,128)(2,1)S(1)} copy-done((bf16[32,7168]{1,0:T(8,128)(2,1)S(1)}, bf16[32,7168]{1,0:T(8,128)(2,1)}, u32[]{:S(2)}) %copy-start) | copy-done | bytes 458776
  3.1 0.0 copy-start.1
  3.1 0.9 copy-done.1
  4.1 0.0 copy-start.2
  4.1 0.8 copy-done.2
  4.9 71.8 %shard_map.86 = (bf16[32,7168]{1,0:T(8,128)(2,1)S(1)}, bf16[32,16,1792]{2,1,0:T(8,128)(2,1)S(1)}, f32[32,1,128]{2,1,0:T(1,128)S(1)}) custom-call(bf16[256,512]{1,0:T(8,128)(2,1)S(1)} %copy-done.1, bf16[512,7168]{1,0:T(8,128)(2,1)} %w_hbm.1, bf16[1,7168]{1,0:T(2,128)(2,1)S(1)} %reshape.37.bias_ref, bf16[32,7168]{1,0:T(8,128)(2,1)S(1)} %copy-done, ...), custom_call_target="tpu_custom_call" | custom-call | flops 1879048192 | bytes 7340032 | tf_op jit(solution)/shard_map/pallas_call | solution.py:269
  76.7 2.3 %reshape.39 = f32[32,4,4,1792]{3,2,1,0:T(4,128)} reshape(bf16[32,16,1792]{2,1,0:T(8,128)(2,1)S(1)} %get-tuple-element.6) | data formatting | bytes 5505024 | tf_op jit(solution)/shard_map/convert_element_type | solution.py:326
  79.0 4.8 %copy.10 = f32[32,4,4,1792]{3,2,1,0:T(4,128)} copy(f32[32,4,4,1792]{3,1,2,0:T(4,128)} %bitcast.4) | data formatting | bytes 7340032 | tf_op jit(solution)/shard_map/convert_element_type | solution.py:326
  83.8 0.0 copy-start.3
  83.8 6.0 %reshape.38 = f32[32,1,2,2,7168]{4,3,2,1,0:T(2,128)} reshape(f32[32,4,4,1792]{3,2,1,0:T(4,128)} %copy.10) | data formatting | bytes 7340032 | tf_op jit(solution)/shard_map/convert_element_type | solution.py:326
  89.8 0.1 copy.11
  89.9 0.1 copy.12
  90.0 0.0 copy-done.3
  90.1 5.2 %multiply_convert_fusion = bf16[32,1,2,2,7168]{4,3,2,1,0:T(2,128)(2,1)} fusion(f32[32,1,2,2,7168]{4,3,2,1,0:T(2,128)} %reshape.38, f32[7168]{0:T(1024)S(1)} %convert_element_type.36, f32[32,2,2]{2,1,0:T(2,128)S(1)} %copy.12), kind=kLoop, calls=%fused_computation | loop fusion | flops 2752512 | bytes 5534208 | tf_op jit(solution)/shard_map/convert_element_type | solution.py:327
  95.2 0.8 copy.14
  (1 shorter events, 0.0 us)
Async XLA Ops:
  2.1 1.0 %copy-start = (bf16[32,7168]{1,0:T(8,128)(2,1)S(1)}, bf16[32,7168]{1,0:T(8,128)(2,1)}, u32[]{:S(2)}) copy-start(bf16[32,7168]{1,0:T(8,128)(2,1)} %res_hbm.1) | copy-start | bytes 1376260
  3.1 0.9 copy-start.1
  4.1 0.8 copy-start.2
  83.8 6.2 %copy-start.3 = (bf16[7168]{0:T(1024)(128)(2,1)S(1)}, bf16[7168]{0:T(1024)(128)(2,1)}, u32[]{:S(2)}) copy-start(bf16[7168]{0:T(1024)(128)(2,1)} %param.12) | copy-start | bytes 43012

commit v2 on v1

--- a/solution.py
+++ b/solution.py
@@ -14,6 +14,7 @@
 F32 = jnp.float32
 
 STRIP = 256
+FINAL = 256
 
 
 def iota(shape, dim):
@@ -22,11 +23,12 @@
 
 def kernel(
     owners, groups, features,
-    ctx_hbm, w_hbm, bias_ref, res_hbm, bits_hbm, routes_ref,
-    hid_hbm, raw_hbm, scl_hbm,
+    ctx_hbm, w_hbm, bias_hbm, res_hbm, bits_hbm, routes_hbm,
+    hid_s, x_recv, scl_r,
     ctx_s, w_s, a_send, a_own, a_recv, b_send, b_recv, b_keep, c_send, c_recv, c_keep,
-    res_s, bits_s, mask_s, hid_s, select_s, slots_s, squares_s, x_send, scl_s,
-    ctx_sem, w_sem, res_sem, bits_sem, hid_sem, own_sem, own_scl_sem,
+    res_s, bits_s, mask_s, select_s, slots_s, squares_s, x_send, scl_s,
+    bias_b, routes_s, bias_s,
+    ctx_sem, w_sem, res_sem, bits_sem, small_sem, own_sem, own_scl_sem,
     a_ssem, a_rsem, b_ssem, b_rsem, c_ssem, c_rsem, x_ssem, x_rsem, s_ssem, s_rsem,
 ):
     quarter = features // 4
@@ -80,6 +82,14 @@
     res_copy.start()
     bits_copy = pltpu.make_async_copy(bits_hbm, bits_s, bits_sem)
     bits_copy.start()
+    small_copies = [
+        pltpu.make_async_copy(src, dst, small_sem.at[i])
+        for i, (src, dst) in enumerate(
+            ((routes_hbm, routes_s), (bias_hbm, bias_b))
+        )
+    ]
+    for copy in small_copies:
+        copy.start()
 
     def matmul(k):
         for q in range(4):
@@ -119,22 +129,22 @@
         c_copy(k).wait_recv()
         pieces = []
         for q in range(4):
-            cols = pl.ds(pl.multiple_of(q * quarter + k * STRIP, 128), STRIP)
-            lanes = pl.ds(q * STRIP, STRIP)
-            total = c_keep[k, :, lanes] + c_recv[k, :, lanes].astype(F32)
-            attention = total.astype(BF16).astype(F32)
-            hidden = (
-                res_s[:, cols].astype(F32)
-                + (attention + bias_ref[:, cols].astype(F32)) * mask_s[:, cols]
-            ).astype(BF16)
-            hid_s[:, cols] = hidden
-            value = hidden.astype(F32)
-            square = value * value
-            folded = square[:, :128]
-            for i in range(1, STRIP // 128):
-                folded = folded + square[:, i * 128:(i + 1) * 128]
-            squares_s[...] += folded
-            pieces.append(hidden)
+            parts = []
+            for i in range(STRIP // 128):
+                block = q * (quarter // 128) + k * (STRIP // 128) + i
+                cols = pl.ds(pl.multiple_of(block * 128, 128), 128)
+                lanes = pl.ds(q * STRIP + i * 128, 128)
+                total = c_keep[k, :, lanes] + c_recv[k, :, lanes].astype(F32)
+                attention = total.astype(BF16).astype(F32)
+                hidden = (
+                    res_s[:, cols].astype(F32)
+                    + (attention + bias_s[pl.ds(block, 1), :]) * mask_s[:, cols]
+                ).astype(BF16)
+                hid_s[:, cols] = hidden
+                value = hidden.astype(F32)
+                squares_s[...] += value * value
+                parts.append(hidden)
+            pieces.append(jnp.concatenate(parts, axis=1))
         stacked = jnp.concatenate(pieces, axis=0)
         picked = jnp.dot(select_s[...], stacked, preferred_element_type=F32).astype(BF16)
         cols = pl.ds(pl.multiple_of(k * STRIP, 128), STRIP)
@@ -144,7 +154,7 @@
         def _(i):
             peer = (expert + i) % owners
             pltpu.make_async_remote_copy(
-                src_ref=x_send.at[peer, :, cols], dst_ref=raw_hbm.at[expert, :, cols],
+                src_ref=x_send.at[peer, :, cols], dst_ref=x_recv.at[expert, :, cols],
                 send_sem=x_ssem, recv_sem=x_rsem,
                 device_id={"expert": peer}, device_id_type=MESH,
             ).start()
@@ -159,12 +169,19 @@
     stage_b(0)
 
     same_token = iota((32, 128), 1) % 32 == iota((32, 128), 0)
-    first = jnp.sum(jnp.where(same_token, routes_ref[:, 0:1], 0), axis=0, keepdims=True)
-    second = jnp.sum(jnp.where(same_token, routes_ref[:, 1:2], 0), axis=0, keepdims=True)
+    for copy in small_copies:
+        copy.wait()
+    named_by = jnp.dot(
+        routes_s[...].astype(F32).astype(BF16),
+        jnp.where(same_token, 1.0, 0.0).astype(BF16),
+        preferred_element_type=F32,
+    )
+    first, second = named_by[0:1], named_by[1:2]
     j0, j1 = iota((128, 128), 0), iota((128, 128), 1)
     before = jnp.where((j0 // 32 == j1 // 32) & (j0 % 32 < j1 % 32), 1.0, 0.0).astype(BF16)
 
     def chosen(named, slot):
+        named = named.astype(F32)
         hits = jnp.where((first == named) | (second == named), 1.0, 0.0)
         earlier = jnp.dot(hits.astype(BF16), before, preferred_element_type=F32)
         return jnp.where(earlier == slot.astype(F32), hits, 0.0)
@@ -177,6 +194,7 @@
         picks = chosen(2 * row + slot // 2, jnp.full((owners, 128), slot % 2, jnp.int32))
         slots_s[slot] = jnp.where(lane < 32, picks, 0.0)
 
+    bias_s[...] = bias_b[...].astype(F32)
     bits_copy.wait()
     squares_s[...] = jnp.zeros_like(squares_s)
     words = features // 16
@@ -230,16 +248,14 @@
     def _(i):
         peer = (expert + i) % owners
         pltpu.make_async_remote_copy(
-            src_ref=scl_s.at[peer], dst_ref=scl_hbm.at[expert],
+            src_ref=scl_s.at[peer], dst_ref=scl_r.at[expert],
             send_sem=s_ssem, recv_sem=s_rsem,
             device_id={"expert": peer}, device_id_type=MESH,
         ).start()
 
-    hid_copy = pltpu.make_async_copy(hid_s, hid_hbm, hid_sem)
-    hid_copy.start()
-    own_copy = pltpu.make_async_copy(x_send.at[expert], raw_hbm.at[expert], own_sem)
+    own_copy = pltpu.make_async_copy(x_send.at[expert], x_recv.at[expert], own_sem)
     own_copy.start()
-    own_scl = pltpu.make_async_copy(scl_s.at[expert], scl_hbm.at[expert], own_scl_sem)
+    own_scl = pltpu.make_async_copy(scl_s.at[expert], scl_r.at[expert], own_scl_sem)
     own_scl.start()
 
     @pl.loop(0, chunks)
@@ -251,11 +267,78 @@
     others = pl.ds(0, owners - 1)
     pltpu.make_async_copy(x_send.at[others], x_send.at[others], x_ssem).wait()
     pltpu.make_async_copy(scl_s.at[others], scl_s.at[others], s_ssem).wait()
-    pltpu.make_async_copy(raw_hbm.at[others], raw_hbm.at[others], x_rsem).wait()
-    pltpu.make_async_copy(scl_hbm.at[others], scl_hbm.at[others], s_rsem).wait()
-    hid_copy.wait()
+    pltpu.make_async_copy(x_recv.at[others], x_recv.at[others], x_rsem).wait()
+    pltpu.make_async_copy(scl_r.at[others], scl_r.at[others], s_rsem).wait()
     own_copy.wait()
     own_scl.wait()
+
+
+def finish(
+    owners, features,
+    hid_hbm, x_hbm, scl_hbm, gain_hbm,
+    hid_out, out_hbm,
+    x_recv, scl_r, gain_b, gain_s, out_s,
+    hid_sem, x_sem, small_sem, out_sem,
+):
+    quarter = features // 4
+    groups = owners // 8
+    hid_copy = pltpu.make_async_copy(hid_hbm, hid_out, hid_sem)
+    scl_copy = pltpu.make_async_copy(scl_hbm, scl_r, small_sem.at[0])
+    gain_copy = pltpu.make_async_copy(gain_hbm, gain_b, small_sem.at[1])
+    x_copies = [
+        pltpu.make_async_copy(x_hbm.at[pl.ds(g * 8, 8)], x_recv.at[pl.ds(g * 8, 8)], x_sem.at[g])
+        for g in range(groups)
+    ]
+    out_copies = [
+        pltpu.make_async_copy(out_s.at[pl.ds(g * 16, 16)], out_hbm.at[pl.ds(g * 16, 16)], out_sem.at[g])
+        for g in range(groups)
+    ]
+    scl_copy.start()
+    gain_copy.start()
+    for copy in x_copies:
+        copy.start()
+    hid_copy.start()
+    gain_copy.wait()
+    gain_s[...] = gain_b[...].astype(F32)
+    scl_copy.wait()
+
+    rows_out = owners * 4
+    spread = jnp.where(iota((rows_out, owners), 0) // 4 == iota((rows_out, owners), 1), 1.0, 0.0)
+    spread = spread.astype(BF16)
+    left = scl_r[...].reshape(owners, 128)
+    per_row = jnp.zeros((rows_out, 128), F32)
+    for _ in range(3):
+        part = left.astype(BF16)
+        left = left - part.astype(F32)
+        per_row = per_row + jnp.dot(spread, part, preferred_element_type=F32)
+    own_lane = iota((rows_out, 128), 1) == iota((rows_out, 128), 0) % 4
+    column = jnp.sum(jnp.where(own_lane, per_row, 0.0), axis=1, keepdims=True)
+    to, came = iota((128, 128), 0), iota((128, 128), 1)
+    source_of = (to % 32) // 4 * 16 + to // 32 * 4 + to % 4
+    reorder = jnp.where(source_of == came, 1.0, 0.0).astype(BF16)
+    for group in range(owners // 8):
+        x_copies[group].wait()
+        scale = jnp.broadcast_to(column[group * 32:group * 32 + 32], (32, 128))
+
+        @pl.loop(0, quarter // FINAL)
+        def _(n):
+            cols = pl.ds(pl.multiple_of(n * FINAL, 128), FINAL)
+            rows = x_recv[group * 8:group * 8 + 8, :, cols].reshape(128, FINAL)
+            moved = jnp.dot(reorder, rows, preferred_element_type=F32)
+            for q in range(4):
+                for i in range(FINAL // 128):
+                    block = q * (quarter // 128) + n * (FINAL // 128) + i
+                    value = moved[q * 32:q * 32 + 32, i * 128:i * 128 + 128]
+                    value = value * scale * gain_s[pl.ds(block, 1), :]
+                    cols_out = pl.ds(pl.multiple_of(block * 128, 128), 128)
+                    out_s[group * 16:group * 16 + 16, :, cols_out] = (
+                        value.astype(BF16).reshape(16, 2, 128)
+                    )
+
+        out_copies[group].start()
+    hid_copy.wait()
+    for copy in out_copies:
+        copy.wait()
 
 
 def local(owners, groups, context, out_weight, attn_bias, residual, dropout_bits, norm_gain, routes):
@@ -266,22 +349,19 @@
     chunks = quarter // STRIP
     wide = 4 * STRIP
     vmem, dma = pltpu.VMEM, pltpu.SemaphoreType.DMA
-    hidden, raw, scales = pl.pallas_call(
+    hidden, sent, scales = pl.pallas_call(
         functools.partial(kernel, owners, groups, features),
         out_shape=(
             jax.ShapeDtypeStruct((tokens, features), BF16),
             jax.ShapeDtypeStruct((owners, 16, quarter), BF16),
             jax.ShapeDtypeStruct((owners, 1, 128), F32),
         ),
-        in_specs=[
-            pl.BlockSpec(memory_space=pl.ANY),
-            pl.BlockSpec(memory_space=pl.ANY),
+        in_specs=[pl.BlockSpec(memory_space=pltpu.HBM)] * 6,
+        out_specs=[
             pl.BlockSpec(memory_space=pltpu.VMEM),
-            pl.BlockSpec(memory_space=pl.ANY),
-            pl.BlockSpec(memory_space=pl.ANY),
-            pl.BlockSpec(memory_space=pltpu.VMEM),
+            pl.BlockSpec(memory_space=pltpu.HBM),
+            pl.BlockSpec(memory_space=pltpu.HBM),
         ],
-        out_specs=[pl.BlockSpec(memory_space=pl.ANY)] * 3,
         scratch_shapes=[
             vmem((rows, depth), BF16),
             vmem((chunks, depth, wide), BF16),
@@ -297,34 +377,54 @@
             vmem((tokens, features), BF16),
             vmem((tokens, features // 16), jnp.int32),
             vmem((tokens, features), F32),
-            vmem((tokens, features), BF16),
             vmem((owners * 16, 128), BF16),
             vmem((4, owners, 128), F32),
             vmem((tokens, 128), F32),
             vmem((owners, 16, quarter), BF16),
             vmem((owners, 1, 128), F32),
+            vmem((features // 128, 128), BF16),
+            vmem((2, tokens), jnp.int32),
+            vmem((features // 128, 128), F32),
             dma((8,)),
             dma((chunks, 4)),
-            dma, dma, dma, dma, dma,
+            dma, dma,
+            dma((2,)),
+            dma, dma,
             dma((chunks,)), dma((chunks,)),
             dma((chunks,)), dma((chunks,)),
             dma((chunks,)), dma((chunks,)),
             dma, dma, dma, dma,
         ],
         compiler_params=pltpu.CompilerParams(
-            collective_id=0, has_side_effects=True, vmem_limit_bytes=48 * 1024 * 1024
+            collective_id=0, has_side_effects=True, vmem_limit_bytes=60 * 1024 * 1024
         ),
         cost_estimate=pl.CostEstimate(
             flops=2 * rows * depth * features,
             bytes_accessed=2 * depth * features,
             transcendentals=0,
         ),
-    )(context, out_weight, attn_bias.reshape(1, -1), residual, dropout_bits, routes)
-    placed = raw.reshape(owners, 4, 4, quarter).transpose(0, 2, 1, 3).reshape(owners, 4, features)
-    scale = scales[:, 0, :4]
-    normed = (
-        placed.astype(F32) * scale[:, :, None] * norm_gain.astype(F32)[None, None, :]
-    ).astype(BF16)
+    )(context, out_weight, attn_bias.reshape(-1, 128), residual, dropout_bits, routes.T)
+    hidden, normed = pl.pallas_call(
+        functools.partial(finish, owners, features),
+        out_shape=(
+            jax.ShapeDtypeStruct((tokens, features), BF16),
+            jax.ShapeDtypeStruct((owners * 2, 2, features), BF16),
+        ),
+        in_specs=[pl.BlockSpec(memory_space=pltpu.HBM)] * 4,
+        out_specs=[pl.BlockSpec(memory_space=pltpu.HBM)] * 2,
+        scratch_shapes=[
+            vmem((owners, 16, quarter), BF16),
+            vmem((owners, 1, 128), F32),
+            vmem((features // 128, 128), BF16),
+            vmem((features // 128, 128), F32),
+            vmem((owners * 2, 2, features), BF16),
+            dma,
+            dma((owners // 8,)),
+            dma((2,)),
+            dma((owners // 8,)),
+        ],
+        compiler_params=pltpu.CompilerParams(vmem_limit_bytes=60 * 1024 * 1024),
+    )(hidden, sent, scales, norm_gain.reshape(-1, 128))
     return hidden, normed.reshape(owners, 1, 2, 2, features)
 
 

time: 96.6 us -> 89 us (0.921)
  local copies, waits for them, and re-layouts: 18.4 us -> 0 us
  Pallas kernels: 71.8 us -> 87.5 us
  other arithmetic: 5.19 us -> 0 us
    pallas_call x0 -> x1, Pallas kernels: none -> 15.1 us  [local(): pl.pallas_call(functools.partial(finish, owners, features), out_shape=(ja...]
    convert_element_type x3 -> x0, local copies, waits for them, and re-layouts: 13.1 us -> none  [local(): placed.astype(F32) * scale[:, :, None]]
    convert_element_type x2 -> x0, other arithmetic: 5.19 us -> none  [the longest x1 5.18 us: local(): normed = (placed.astype(F32) * scale[:, :, None] * norm_gain.astype(F32)[...]
    unnamed x10 -> x0, local copies, waits for them, and re-layouts: 4.34 us -> none
where the time goes in v2:
time: 89 us; the launch traced here: 88.1 us
  Pallas kernels  87.5 us (98%)
    pallas_call x1, Pallas kernels, local(): pl.pallas_call(functools.partial(kernel, owners, groups, features), out_s...  72.3 us
    pallas_call x1, Pallas kernels, local(): pl.pallas_call(functools.partial(finish, owners, features), out_shape=(ja...  15.1 us

profile of v2, /device:TPU:1, one launch (start us, length us, event | category | flops | bytes accessed | tf_op | source)
XLA Modules:
  0.0 88.1 jit_solution(14375592856225660582)
XLA Ops:
  0.6 72.3 %shard_map.86 = (bf16[32,7168]{1,0:T(8,128)(2,1)}, bf16[32,16,1792]{2,1,0:T(8,128)(2,1)}, f32[32,1,128]{2,1,0:T(1,128)}) custom-call(bf16[256,512]{1,0:T(8,128)(2,1)} %ctx_hbm.1, bf16[512,7168]{1,0:T(8,128)(2,1)} %w_hbm.1, bf16[56,128]{1,0:T(8,128)(2,1)} %bitcast.6, bf16[32,7168]{1,0:T(8,128)(2,1)} %res_hbm.1, s32[32,448]{1,0:T(8,128)} %bits_hbm.1, ...), custom_call_target="tpu_custom_call" | custom-call | flops 1879048192 | bytes 7340032 | tf_op jit(solution)/shard_map/pallas_call | solution.py:352
  73.0 15.1 %shard_map.87 = (bf16[32,7168]{1,0:T(8,128)(2,1)}, bf16[64,2,7168]{2,1,0:T(2,128)(2,1)}) custom-call(bf16[32,7168]{1,0:T(8,128)(2,1)} %get-tuple-element.7.hid_hbm, bf16[32,16,1792]{2,1,0:T(8,128)(2,1)} %get-tuple-element.8.x_hbm, f32[32,1,128]{2,1,0:T(1,128)} %get-tuple-element.9.scl_hbm, bf16[56,128]{1,0:T(8,128)(2,1)} %bitcast.7), custom_call_target="tpu_custom_call" | custom-call | tf_op jit(solution)/shard_map/pallas_call | solution.py:407

commit v3 on v2

--- a/solution.py
+++ b/solution.py
@@ -277,12 +277,13 @@
     owners, features,
     hid_hbm, x_hbm, scl_hbm, gain_hbm,
     hid_out, out_hbm,
-    x_recv, scl_r, gain_b, gain_s, out_s,
+    x_recv, scl_r, gain_b, gain_s, out_s, hid_v,
     hid_sem, x_sem, small_sem, out_sem,
 ):
     quarter = features // 4
     groups = owners // 8
-    hid_copy = pltpu.make_async_copy(hid_hbm, hid_out, hid_sem)
+    hid_in = pltpu.make_async_copy(hid_hbm, hid_v, hid_sem.at[0])
+    hid_copy = pltpu.make_async_copy(hid_v, hid_out, hid_sem.at[1])
     scl_copy = pltpu.make_async_copy(scl_hbm, scl_r, small_sem.at[0])
     gain_copy = pltpu.make_async_copy(gain_hbm, gain_b, small_sem.at[1])
     x_copies = [
@@ -297,10 +298,12 @@
     gain_copy.start()
     for copy in x_copies:
         copy.start()
-    hid_copy.start()
+    hid_in.start()
     gain_copy.wait()
     gain_s[...] = gain_b[...].astype(F32)
     scl_copy.wait()
+    hid_in.wait()
+    hid_copy.start()
 
     rows_out = owners * 4
     spread = jnp.where(iota((rows_out, owners), 0) // 4 == iota((rows_out, owners), 1), 1.0, 0.0)
@@ -320,7 +323,7 @@
         x_copies[group].wait()
         scale = jnp.broadcast_to(column[group * 32:group * 32 + 32], (32, 128))
 
-        @pl.loop(0, quarter // FINAL)
+        @pl.loop(0, quarter // FINAL, unroll=True)
         def _(n):
             cols = pl.ds(pl.multiple_of(n * FINAL, 128), FINAL)
             rows = x_recv[group * 8:group * 8 + 8, :, cols].reshape(128, FINAL)
@@ -418,7 +421,8 @@
             vmem((features // 128, 128), BF16),
             vmem((features // 128, 128), F32),
             vmem((owners * 2, 2, features), BF16),
-            dma,
+            vmem((tokens, features), BF16),
+            dma((2,)),
             dma((owners // 8,)),
             dma((2,)),
             dma((owners // 8,)),

time: 89 us -> 78.7 us (0.88)
  Pallas kernels: 87.5 us -> 77.1 us
    pallas_call x1, Pallas kernels: 15.1 us -> 4.75 us  [local(): pl.pallas_call(functools.partial(finish, owners, features), out_shape=(ja...]
where the time goes in v3:
time: 78.7 us; the launch traced here: 77.7 us
  Pallas kernels  77.1 us (98%)
    pallas_call x1, Pallas kernels, local(): pl.pallas_call(functools.partial(kernel, owners, groups, features), out_s...  72.3 us
    pallas_call x1, Pallas kernels, local(): pl.pallas_call(functools.partial(finish, owners, features), out_shape=(ja...  4.75 us

profile of v3, /device:TPU:1, one launch (start us, length us, event | category | flops | bytes accessed | tf_op | source)
XLA Modules:
  0.0 77.7 jit_solution(12283573165119736787)
XLA Ops:
  0.6 72.3 %shard_map.86 = (bf16[32,7168]{1,0:T(8,128)(2,1)}, bf16[32,16,1792]{2,1,0:T(8,128)(2,1)}, f32[32,1,128]{2,1,0:T(1,128)}) custom-call(bf16[256,512]{1,0:T(8,128)(2,1)} %ctx_hbm.1, bf16[512,7168]{1,0:T(8,128)(2,1)} %w_hbm.1, bf16[56,128]{1,0:T(8,128)(2,1)} %bitcast.6, bf16[32,7168]{1,0:T(8,128)(2,1)} %res_hbm.1, s32[32,448]{1,0:T(8,128)} %bits_hbm.1, ...), custom_call_target="tpu_custom_call" | custom-call | flops 1879048192 | bytes 7340032 | tf_op jit(solution)/shard_map/pallas_call | solution.py:355
  73.0 4.8 %shard_map.87 = (bf16[32,7168]{1,0:T(8,128)(2,1)}, bf16[64,2,7168]{2,1,0:T(2,128)(2,1)}) custom-call(bf16[32,7168]{1,0:T(8,128)(2,1)} %get-tuple-element.7.hid_hbm, bf16[32,16,1792]{2,1,0:T(8,128)(2,1)} %get-tuple-element.8.x_hbm, f32[32,1,128]{2,1,0:T(1,128)} %get-tuple-element.9.scl_hbm, bf16[56,128]{1,0:T(8,128)(2,1)} %bitcast.7), custom_call_target="tpu_custom_call" | custom-call | tf_op jit(solution)/shard_map/pallas_call | solution.py:410

commit v4 on v3

--- a/solution.py
+++ b/solution.py
@@ -150,6 +150,9 @@
         cols = pl.ds(pl.multiple_of(k * STRIP, 128), STRIP)
         x_send[:, :, cols] = picked.reshape(owners, 16, STRIP)
 
+    def dispatch(first, width):
+        cols = pl.ds(pl.multiple_of(first, 128), width)
+
         @pl.loop(1, owners)
         def _(i):
             peer = (expert + i) % owners
@@ -221,6 +224,14 @@
         @pl.when(t >= 1)
         def _():
             stage_x(t - 1)
+
+        @pl.when(t == 1)
+        def _():
+            dispatch(0, STRIP)
+
+        @pl.when((t > 1) & (t % 2 == 1))
+        def _():
+            dispatch((t - 2) * STRIP, 2 * STRIP)
 
         @pl.when(t < chunks)
         def _():

time: 78.7 us -> 84.3 us (1.071)
  Pallas kernels: 77.1 us -> 83.4 us
    pallas_call x1, Pallas kernels: 72.3 us -> 78.7 us  [local(): pl.pallas_call(functools.partial(kernel, owners, groups, features), out_s...]
where the time goes in v4:
time: 84.3 us; the launch traced here: 84.1 us
  Pallas kernels  83.4 us (99%)
    pallas_call x1, Pallas kernels, local(): pl.pallas_call(functools.partial(kernel, owners, groups, features), out_s...  78.7 us
    pallas_call x1, Pallas kernels, local(): pl.pallas_call(functools.partial(finish, owners, features), out_shape=(ja...  4.75 us

profile of v4, /device:TPU:1, one launch (start us, length us, event | category | flops | bytes accessed | tf_op | source)
XLA Modules:
  0.0 84.1 jit_solution(15999757221790263691)
XLA Ops:
  0.6 78.7 %shard_map.86 = (bf16[32,7168]{1,0:T(8,128)(2,1)}, bf16[32,16,1792]{2,1,0:T(8,128)(2,1)}, f32[32,1,128]{2,1,0:T(1,128)}) custom-call(bf16[256,512]{1,0:T(8,128)(2,1)} %ctx_hbm.1, bf16[512,7168]{1,0:T(8,128)(2,1)} %w_hbm.1, bf16[56,128]{1,0:T(8,128)(2,1)} %bitcast.6, bf16[32,7168]{1,0:T(8,128)(2,1)} %res_hbm.1, s32[32,448]{1,0:T(8,128)} %bits_hbm.1, ...), custom_call_target="tpu_custom_call" | custom-call | flops 1879048192 | bytes 7340032 | tf_op jit(solution)/shard_map/pallas_call | solution.py:366
  79.3 4.8 %shard_map.87 = (bf16[32,7168]{1,0:T(8,128)(2,1)}, bf16[64,2,7168]{2,1,0:T(2,128)(2,1)}) custom-call(bf16[32,7168]{1,0:T(8,128)(2,1)} %get-tuple-element.7.hid_hbm, bf16[32,16,1792]{2,1,0:T(8,128)(2,1)} %get-tuple-element.8.x_hbm, f32[32,1,128]{2,1,0:T(1,128)} %get-tuple-element.9.scl_hbm, bf16[56,128]{1,0:T(8,128)(2,1)} %bitcast.7), custom_call_target="tpu_custom_call" | custom-call | tf_op jit(solution)/shard_map/pallas_call | solution.py:421

commit v5 on v3

--- a/solution.py
+++ b/solution.py
@@ -216,15 +216,15 @@
         mask_s[:, start * 16:(start + count) * 16] = bit.astype(F32) * KEEP_SCALE
     res_copy.wait()
 
-    @pl.loop(0, chunks + 1)
+    @pl.loop(0, chunks + 2)
     def _(t):
-        @pl.when(t >= 1)
+        @pl.when(t >= 2)
         def _():
-            stage_x(t - 1)
-
-        @pl.when(t < chunks)
+            stage_x(t - 2)
+
+        @pl.when((t >= 1) & (t <= chunks))
         def _():
-            stage_c(t)
+            stage_c(t - 1)
 
         @pl.when(t + 1 < chunks)
         def _():

time: 78.7 us -> 80.1 us (1.018); the launches traced: 77.7 us -> 80 us
  Pallas kernels: 77.1 us -> 79.3 us
    pallas_call x1, Pallas kernels: 72.3 us -> 74.6 us  [local(): pl.pallas_call(functools.partial(kernel, owners, groups, features), out_s...]
where the time goes in v5:
time: 80.1 us; the launch traced here: 80 us
  Pallas kernels  79.3 us (99%)
    pallas_call x1, Pallas kernels, local(): pl.pallas_call(functools.partial(kernel, owners, groups, features), out_s...  74.6 us
    pallas_call x1, Pallas kernels, local(): pl.pallas_call(functools.partial(finish, owners, features), out_shape=(ja...  4.75 us

profile of v5, /device:TPU:1, one launch (start us, length us, event | category | flops | bytes accessed | tf_op | source)
XLA Modules:
  0.0 80.0 jit_solution(5576849866334653579)
XLA Ops:
  0.6 74.6 %shard_map.86 = (bf16[32,7168]{1,0:T(8,128)(2,1)}, bf16[32,16,1792]{2,1,0:T(8,128)(2,1)}, f32[32,1,128]{2,1,0:T(1,128)}) custom-call(bf16[256,512]{1,0:T(8,128)(2,1)} %ctx_hbm.1, bf16[512,7168]{1,0:T(8,128)(2,1)} %w_hbm.1, bf16[56,128]{1,0:T(8,128)(2,1)} %bitcast.6, bf16[32,7168]{1,0:T(8,128)(2,1)} %res_hbm.1, s32[32,448]{1,0:T(8,128)} %bits_hbm.1, ...), custom_call_target="tpu_custom_call" | custom-call | flops 1879048192 | bytes 7340032 | tf_op jit(solution)/shard_map/pallas_call | solution.py:355
  75.2 4.8 %shard_map.87 = (bf16[32,7168]{1,0:T(8,128)(2,1)}, bf16[64,2,7168]{2,1,0:T(2,128)(2,1)}) custom-call(bf16[32,7168]{1,0:T(8,128)(2,1)} %get-tuple-element.7.hid_hbm, bf16[32,16,1792]{2,1,0:T(8,128)(2,1)} %get-tuple-element.8.x_hbm, f32[32,1,128]{2,1,0:T(1,128)} %get-tuple-element.9.scl_hbm, bf16[56,128]{1,0:T(8,128)(2,1)} %bitcast.7), custom_call_target="tpu_custom_call" | custom-call | tf_op jit(solution)/shard_map/pallas_call | solution.py:410
